TPU v7x, 32 devices: a whole 2x2x4 slice. The times are simulated.
32 devices in a mesh: src: 16 (over z, y, core), tgt: 2 (over x).
Axes of the slice: x: 2, y: 2, z: 4, core: 2. Of those that a mesh axis runs over, the one named last changes fastest.
Arguments:
- atom_feats: bfloat16 [256, 3200], P(('src', 'tgt')), may hold values from -6 to 6
- positions: float32 [3, 256], P(None, ('src', 'tgt')), may hold values from 0 to 1
- edge_src: int32 [32768], P(('src', 'tgt')), may hold values from 0 to 15
- edge_tgt: int32 [32768], P(('src', 'tgt')), may hold values from 0 to 127
- edge_angle: float32 [32768], P(('src', 'tgt')), may hold values from -3.140625 to 3.140625
- edge_scale: float32 [32768], P(('src', 'tgt')), may hold values from 0.1 to 1
- edge_count: int32 [16, 2], replicated, may hold values from 1 to 1024, as said below
- k_index: int32 [3, 2048], replicated, may hold values from -6 to 6
- k_filter: float32 [2048, 128], replicated, may hold values from -6 to 6
- weight_zero: bfloat16 [2, 640, 640], replicated, may hold values from -0.25 to 0.25
- weight_first: bfloat16 [2, 2, 512, 512], replicated, may hold values from -0.1875 to 0.1875
- weight_second: bfloat16 [2, 2, 384, 384], replicated, may hold values from -0.21875 to 0.21875
- weight_third: bfloat16 [2, 2, 256, 256], replicated, may hold values from -0.25 to 0.25
- weight_fourth: bfloat16 [2, 2, 128, 128], replicated, may hold values from -0.375 to 0.375
Outputs:
- edge_update: bfloat16 [256, 3200], P(('tgt', 'src'))
- long_range: float32 [256, 128], P(('src', 'tgt'))
Inputs may be any that keep to these rules, and one draw needn't show every extreme that they name: `edge_count`: live edge slots of tile (s, t); in every draw some tile is full with 1024.
All inputs are finite; a program needn't handle non-finite values.
Results may differ from a plain program's by a relative error of at most 0.0047.
Values may be sent and summed in bfloat16 or wider, within the bound.
A program may use at most 64 MiB of HBM per device.

v0:
```python
import math

import jax
import jax.numpy as jnp
from jax import lax
from jax.sharding import PartitionSpec as P


def rotate(values, angles, handed, channels, degrees):
    pieces = [values[:, : (degrees + 1) * channels]]
    offset = (degrees + 1) * channels
    for degree in range(1, degrees + 1):
        columns = (degrees + 1 - degree) * channels
        cosine = jnp.cos(degree * angles)[:, None]
        sine_part = handed * jnp.sin(degree * angles)[:, None]
        leading = values[:, offset : offset + columns]
        trailing = values[:, offset + columns : offset + 2 * columns]
        pieces.append(cosine * leading + sine_part * trailing)
        pieces.append(cosine * trailing - sine_part * leading)
        offset += 2 * columns
    return jnp.concatenate(pieces, axis=1)


def pair_matrix(weights, conv_index):
    upper_half = jnp.concatenate([weights[conv_index, 0], weights[conv_index, 1]], axis=1)
    lower_half = jnp.concatenate([-weights[conv_index, 1], weights[conv_index, 0]], axis=1)
    return jnp.concatenate([upper_half, lower_half], axis=0)


def convolve(inputs, matrices):
    outputs = []
    offset = 0
    for matrix in matrices:
        height = matrix.shape[0]
        outputs.append(
            jnp.dot(inputs[:, offset : offset + height], matrix, preferred_element_type=jnp.float32)
        )
        offset += height
    return jnp.concatenate(outputs, axis=1)


def phase_table(coords, k_index):
    k_float = k_index.astype(jnp.float32)
    return (
        2.0
        * math.pi
        * (
            coords[0][:, None] * k_float[0][None, :]
            + coords[1][:, None] * k_float[1][None, :]
            + coords[2][:, None] * k_float[2][None, :]
        )
    )


def highest_dot(left_side, right_side):
    return jnp.dot(
        left_side, right_side, precision=lax.Precision.HIGHEST, preferred_element_type=jnp.float32
    )


def body(
    atom_feats,
    positions,
    edge_src,
    edge_tgt,
    edge_angle,
    edge_scale,
    edge_count,
    k_index,
    k_filter,
    weight_zero,
    weight_first,
    weight_second,
    weight_third,
    weight_fourth,
):
    channels = k_filter.shape[1]
    degrees = 4
    capacity = edge_src.shape[0]
    source_count = lax.axis_size("src")
    target_count = lax.axis_size("tgt")
    own_atoms = atom_feats.shape[0]
    target_rows = own_atoms * source_count
    feat_columns = atom_feats.shape[1]
    source_group = lax.axis_index("src")
    target_group = lax.axis_index("tgt")
    sections = []
    for conv_index in (0, 1):
        sections.append(
            [weight_zero[conv_index]]
            + [
                pair_matrix(weights, conv_index)
                for weights in (weight_first, weight_second, weight_third, weight_fourth)
            ]
        )
    block_feats = lax.all_gather(atom_feats, "tgt", axis=0, tiled=True)
    step_rows = math.gcd(256, capacity // 2)
    lane_ids = jnp.arange(step_rows, dtype=jnp.int32)
    target_ids = jnp.arange(target_rows, dtype=jnp.int32)

    def edge_message(edge_rows, angles, scales):
        turned = rotate(edge_rows.astype(jnp.float32), angles, 1.0, channels, degrees).astype(
            jnp.bfloat16
        )
        hidden = jax.nn.gelu(convolve(turned, sections[0]), approximate=False).astype(jnp.bfloat16)
        second = convolve(hidden, sections[1])
        return rotate(second, angles, -1.0, channels, degrees) * scales[:, None]

    def own_rows(first_slot):
        return jnp.take(
            block_feats, lax.dynamic_slice_in_dim(edge_src, first_slot, step_rows), axis=0
        )

    count_here = edge_count[source_group, target_group]
    zeros_total = jnp.zeros((target_rows, feat_columns), jnp.float32)

    def one_block(block_number, carried):
        first_slot = block_number * step_rows
        edge_rows = own_rows(first_slot)
        angles = lax.dynamic_slice_in_dim(edge_angle, first_slot, step_rows)
        scales = lax.dynamic_slice_in_dim(edge_scale, first_slot, step_rows)
        targets = lax.dynamic_slice_in_dim(edge_tgt, first_slot, step_rows)
        slot_ids = first_slot + lane_ids
        live_mask = ((slot_ids >= 0) & (slot_ids < count_here)).astype(jnp.float32)
        messages = edge_message(edge_rows, angles, scales) * live_mask[:, None]
        one_hot = (targets[:, None] == target_ids[None, :]).astype(jnp.float32)
        added = lax.dot_general(
            one_hot,
            messages,
            (((0,), (0,)), ((), ())),
            precision=lax.Precision.HIGHEST,
            preferred_element_type=jnp.float32,
        )
        return carried + added

    totals = lax.fori_loop(0, (count_here + step_rows - 1) // step_rows, one_block, zeros_total)
    edge_update = lax.psum_scatter(totals, "src", scatter_dimension=0, tiled=True).astype(
        jnp.bfloat16
    )
    total_atoms = own_atoms * source_count * target_count
    norm_factor = 1.0 / math.sqrt(total_atoms * k_filter.shape[0])
    phase = phase_table(positions, k_index)
    cos_table = jnp.cos(phase)
    sin_table = jnp.sin(phase)
    charges = atom_feats[:, :channels].astype(jnp.float32)
    factors_cos, factors_sin = lax.psum(
        (highest_dot(cos_table.T, charges), highest_dot(sin_table.T, charges)), ("src", "tgt")
    )
    summed = highest_dot(cos_table, k_filter * factors_cos) + highest_dot(
        sin_table, k_filter * factors_sin
    )
    long_range = summed * norm_factor
    return (edge_update, long_range)


def solution(mesh):
    return jax.shard_map(
        body,
        mesh=mesh,
        in_specs=(
            P(("src", "tgt"), None),
            P(None, ("src", "tgt")),
            P(("src", "tgt")),
            P(("src", "tgt")),
            P(("src", "tgt")),
            P(("src", "tgt")),
            P(),
            P(),
            P(),
            P(),
            P(),
            P(),
            P(),
            P(),
        ),
        out_specs=(P(("tgt", "src"), None), P(("src", "tgt"), None)),
        check_vma=False,
    )
```

profile of v0, /device:TPU:0, one launch (start us, length us, event | category | flops | bytes accessed | tf_op | source)
XLA Modules:
  0.0 245.3 jit_solution(6516566817206618018)
XLA Ops:
  7.2 0.8 slice_bitcast_fusion.20
  8.0 0.9 convert_element_type.23
  9.0 2.9 %fusion.55 = f32[2048,128]{1,0:T(8,128)} fusion(f32[2048]{0:T(1024)S(1)} %bitcast.97, f32[8]{0:T(128)S(1)} %get-tuple-element.248, f32[2048]{0:T(1024)S(1)} %bitcast.101, f32[8]{0:T(128)S(1)} %get-tuple-element.249, f32[2048]{0:T(1024)S(1)} %bitcast.93, f32[8]{0:T(128)S(1)} %get-tuple-element.247, bf16[8,3200]{1,0:T(8,128)(2,1)} %param.16), kind=kOutput, calls=%fused_computation.125 | convolution fusion | flops 25264128 | bytes 1075296 | tf_op jit(solution)/shard_map/dot_general | solution.py:56
  11.8 2.8 %fusion.52 = f32[2048,128]{1,0:T(8,128)} fusion(f32[2048]{0:T(1024)S(1)} %bitcast.98, f32[8]{0:T(128)S(1)} %get-tuple-element.248, f32[2048]{0:T(1024)S(1)} %bitcast.102, f32[8]{0:T(128)S(1)} %get-tuple-element.249, f32[2048]{0:T(1024)S(1)} %bitcast.94, f32[8]{0:T(128)S(1)} %get-tuple-element.247, bf16[8,3200]{1,0:T(8,128)(2,1)} %param.16), kind=kOutput, calls=%fused_computation.124 | convolution fusion | flops 25264128 | bytes 1075296 | tf_op jit(solution)/shard_map/dot_general | solution.py:56
  15.9 6.0 %all_gather.3 = bf16[16,3200]{1,0:T(8,128)(2,1)S(1)} all-gather(bf16[8,3200]{1,0:T(8,128)(2,1)} %param.16), channel_id=1, replica_groups=mesh['src'=16,'tgt'=2] {'tgt'}, dimensions={0}, use_global_device_ids=true | all-gather | bytes 153600 | tf_op jit(solution)/shard_map/all_gather | solution.py:96
  22.5 0.7 slice_bitcast_fusion.14
  23.2 1.7 fusion.94
  24.9 1.9 slice_bitcast_fusion.10
  26.8 0.9 fusion.96
  27.7 1.1 slice_bitcast_fusion.6
  28.9 1.4 slice_bitcast_fusion.2
  30.3 2.8 %slice_bitcast_fusion = (bf16[640,640]{1,0:T(8,128)(2,1)}, bf16[640,640]{1,0:T(8,128)(2,1)}) fusion(bf16[2,640,640]{2,1,0:T(8,128)(2,1)} %param.25), kind=kLoop, calls=%fused_computation.102 | loop fusion | bytes 3276800 | tf_op jit(solution)/shard_map/squeeze | solution.py:90
  33.1 1.7 maximum_maximum_fusion.6
  34.8 2.3 maximum_maximum_fusion.4
  37.1 3.2 %maximum_maximum_fusion.2 = (bf16[768,768]{1,0:T(8,128)(2,1)}, bf16[768,768]{1,0:T(8,128)(2,1)}) fusion(bf16[384,384]{1,0:T(8,128)(2,1)} %get-tuple-element.228, bf16[384,384]{1,0:T(8,128)(2,1)} %get-tuple-element.231, bf16[384,384]{1,0:T(8,128)(2,1)} %get-tuple-element.227, bf16[384,384]{1,0:T(8,128)(2,1)} %get-tuple-element.229, ...), kind=kLoop, calls=%fused_computation.95 | loop fusion | flops 9437184 | bytes 4128768 | tf_op jit(solution)/shard_map/concatenate | solution.py:27
  40.3 10.6 %maximum_maximum_fusion = (bf16[1024,1024]{1,0:T(8,128)(2,1)}, bf16[1024,1024]{1,0:T(8,128)(2,1)}) fusion(bf16[512,512]{1,0:T(8,128)(2,1)S(1)} %copy-done.14, bf16[512,512]{1,0:T(8,128)(2,1)S(1)} %get-tuple-element.223, bf16[512,512]{1,0:T(8,128)(2,1)S(1)} %copy-done.13, bf16[512,512]{1,0:T(8,128)(2,1)S(1)} %copy-done.15, ...), kind=kLoop, calls=%fused_computation.93 | loop fusion | flops 16777216 | bytes 7340032 | tf_op jit(solution)/shard_map/concatenate | solution.py:27
  51.1 27.0 %while.11 = (s32[]{:T(128)}, f32[128,3200]{1,0:T(8,128)S(1)}, s32[]{:T(128)}, s32[1024]{0:T(1024)}, s32[1024]{0:T(1024)}, /*index=5*/bf16[16,3200]{1,0:T(8,128)(...) while((s32[]{:T(128)}, f32[128,3200]{1,0:T(8,128)S(1)}, ...), condition=%wide.region_1.2_spmd.clone, body=%wide.region_0.1_spmd.clone.sunk | while | flops 3755169536 | bytes 89998520 | solution.py:136
  51.3 1.3 dynamic_slice.27
  52.6 1.3 dynamic_slice.28
  53.9 2.0 compare_and_fusion.2
  55.9 0.8 broadcast_multiply_fusion.7
  57.9 1.9 gather_fusion
  59.9 1.1 fusion.159
  62.9 0.7 convolution_dynamic-update-slice_fusion.13
  64.6 7.2 %fusion.160 = bf16[256,3200]{1,0:T(8,128)(2,1)S(1)} fusion(f32[256,3200]{1,0:T(8,128)S(1)} %convolution_dynamic-update-slice_fusion.16), kind=kLoop, calls=%fused_computation.7.clone.1 | loop fusion | flops 53248000 | bytes 4915200 | tf_op jit(solution)/shard_map/while/body/convert_element_type | solution.py:105
  73.4 0.7 fusion.161
  75.8 2.2 convolution_add_fusion.3
  78.1 1.3 dynamic-slice
  80.1 152.0 %all-reduce.6 = bf16[128,3200]{1,0:T(8,128)(2,1)} all-reduce(f32[128,3200]{1,0:T(8,128)S(1)} %get-tuple-element.110), channel_id=2, replica_groups=mesh['src'=16,'tgt'=2] {'src'}, use_global_device_ids=true, to_apply=%region_2.3.clone | all-reduce | flops 409600 | bytes 2457600
  232.1 1.4 dynamic-slice_convert_fusion
  233.5 2.2 fusion.47
  235.7 2.8 %fusion.45 = f32[8,128]{1,0:T(8,128)} fusion(f32[8,128]{1,0:T(8,128)S(1)} %fusion.47, f32[2048,128]{1,0:T(8,128)S(1)} %copy-done.9, f32[2048,128]{1,0:T(8,128)} %get-tuple-element.192, f32[2048]{0:T(1024)S(1)} %bitcast.100, f32[8]{0:T(128)S(1)} %copy-done.32, f32[2048]{0:T(1024)S(1)} %bitcast.104, f32[8]{0:T(128)S(1)} %copy-done.34, f32[2048]{0:T(1024)S(1)} %bitcast.96, ...), kind=kOutput, calls=%fused_computation.98 | convolution fusion | flops 25528320 | bytes 2130016 | tf_op jit(solution)/shard_map/dot_general | solution.py:56
  (103 shorter events, 8.7 us)
Async XLA Ops:
  7.2 7.5 %copy-start.35 = (s32[16,2]{0,1:T(2,128)S(1)}, s32[16,2]{0,1:T(2,128)}, u32[]{:S(2)}) copy-start(s32[16,2]{0,1:T(2,128)} %param.22) | copy-start | bytes 388
  7.2 14.7 %copy-start.17 = (bf16[2,2,128,128]{3,2,1,0:T(8,128)(2,1)S(1)}, bf16[2,2,128,128]{3,2,1,0:T(8,128)(2,1)}, u32[]{:S(2)}) copy-start(bf16[2,2,128,128]{3,2,1,0:T(8,128)(2,1)} %param.29) | copy-start | bytes 393220
  7.2 226.3 %all-reduce.5.cloned.1.call-start = ((), (), s32[]{:S(2)}) async-start(), calls=%async_computation | async-start | bytes 4194304 | tf_op jit(solution)/shard_map/psum | solution.py:146
  8.0 18.7 %copy-start.29 = (f32[8]{0:T(128)}, f32[8]{0:T(128)S(1)}, u32[]{:S(2)}) copy-start(f32[8]{0:T(128)S(1)} %get-tuple-element.247) | copy-start | bytes 100
  8.0 18.7 %copy-start.31 = (f32[8]{0:T(128)}, f32[8]{0:T(128)S(1)}, u32[]{:S(2)}) copy-start(f32[8]{0:T(128)S(1)} %get-tuple-element.248) | copy-start | bytes 100
  8.0 18.7 %copy-start.33 = (f32[8]{0:T(128)}, f32[8]{0:T(128)S(1)}, u32[]{:S(2)}) copy-start(f32[8]{0:T(128)S(1)} %get-tuple-element.249) | copy-start | bytes 100
  8.0 18.7 %copy-start.10 = (bf16[2,2,384,384]{3,2,1,0:T(8,128)(2,1)S(1)}, bf16[2,2,384,384]{3,2,1,0:T(8,128)(2,1)}, u32[]{:S(2)}) copy-start(bf16[2,2,384,384]{3,2,1,0:T(8,128)(2,1)} %param.27) | copy-start | bytes 3538948
  8.9 18.7 %copy-start.18 = (f32[1,2048]{1,0:T(1,128)}, f32[1,2048]{1,0:T(1,128)S(1)}, u32[]{:S(2)}) copy-start(f32[1,2048]{1,0:T(1,128)S(1)} %get-tuple-element.245) | copy-start | bytes 24580
  8.9 18.7 %copy-start.20 = (f32[1,2048]{1,0:T(1,128)}, f32[1,2048]{1,0:T(1,128)S(1)}, u32[]{:S(2)}) copy-start(f32[1,2048]{1,0:T(1,128)S(1)} %get-tuple-element.246) | copy-start | bytes 24580
  14.6 14.1 %copy-start.7 = (bf16[2,2,512,512]{3,2,1,0:T(8,128)(2,1)S(1)}, bf16[2,2,512,512]{3,2,1,0:T(8,128)(2,1)}, u32[]{:S(2)}) copy-start(bf16[2,2,512,512]{3,2,1,0:T(8,128)(2,1)} %param.26) | copy-start | bytes 6291460
  28.8 4.2 %copy-start.22 = (bf16[128,128]{1,0:T(8,128)(2,1)S(1)}, bf16[128,128]{1,0:T(8,128)(2,1)}, u32[]{:S(2)}) copy-start(bf16[128,128]{1,0:T(8,128)(2,1)} %get-tuple-element.242) | copy-start | bytes 98308
  28.9 5.9 %copy-start.16 = (bf16[256,256]{1,0:T(8,128)(2,1)S(1)}, bf16[256,256]{1,0:T(8,128)(2,1)}, u32[]{:S(2)}) copy-start(bf16[256,256]{1,0:T(8,128)(2,1)} %get-tuple-element.236) | copy-start | bytes 393220
  33.1 7.3 %copy-start.12 = (bf16[512,512]{1,0:T(8,128)(2,1)S(1)}, bf16[512,512]{1,0:T(8,128)(2,1)}, u32[]{:S(2)}) copy-start(bf16[512,512]{1,0:T(8,128)(2,1)} %get-tuple-element.218) | copy-start | bytes 1572868
  33.1 7.3 %copy-start.13 = (bf16[512,512]{1,0:T(8,128)(2,1)S(1)}, bf16[512,512]{1,0:T(8,128)(2,1)}, u32[]{:S(2)}) copy-start(bf16[512,512]{1,0:T(8,128)(2,1)} %get-tuple-element.219) | copy-start | bytes 1572868
  33.1 7.3 %copy-start.14 = (bf16[512,512]{1,0:T(8,128)(2,1)S(1)}, bf16[512,512]{1,0:T(8,128)(2,1)}, u32[]{:S(2)}) copy-start(bf16[512,512]{1,0:T(8,128)(2,1)} %get-tuple-element.220) | copy-start | bytes 1572868
  33.1 7.3 %copy-start.15 = (bf16[512,512]{1,0:T(8,128)(2,1)S(1)}, bf16[512,512]{1,0:T(8,128)(2,1)}, u32[]{:S(2)}) copy-start(bf16[512,512]{1,0:T(8,128)(2,1)} %get-tuple-element.221) | copy-start | bytes 1572868
  59.9 1.3 copy-start.27
  59.9 1.4 copy-start.26
  61.0 1.9 copy-start.11
  61.5 2.1 copy-start.1
  62.9 1.2 copy-start.5
  64.1 7.7 %copy-start.8 = (bf16[256,256]{1,0:T(8,128)(2,1)S(1)}, bf16[256,256]{1,0:T(8,128)(2,1)}, u32[]{:S(2)}) copy-start(bf16[256,256]{1,0:T(8,128)(2,1)} %get-tuple-element.486) | copy-start | bytes 393220 | tf_op jit(solution)/shard_map/while
  64.4 7.6 %copy-start.6 = (bf16[512,512]{1,0:T(8,128)(2,1)S(1)}, bf16[512,512]{1,0:T(8,128)(2,1)}, u32[]{:S(2)}) copy-start(bf16[512,512]{1,0:T(8,128)(2,1)} %get-tuple-element.485) | copy-start | bytes 1572868 | tf_op jit(solution)/shard_map/while
  64.6 7.7 %copy-start.2 = (bf16[768,768]{1,0:T(8,128)(2,1)S(1)}, bf16[768,768]{1,0:T(8,128)(2,1)}, u32[]{:S(2)}) copy-start(bf16[768,768]{1,0:T(8,128)(2,1)} %get-tuple-element.484) | copy-start | bytes 3538948 | tf_op jit(solution)/shard_map/while
  71.8 1.6 copy-start
  72.3 1.8 copy-start.3
  78.0 155.5 %copy-start.9 = (f32[2048,128]{1,0:T(8,128)S(1)}, f32[2048,128]{1,0:T(8,128)}, u32[]{:S(2)}) copy-start(f32[2048,128]{1,0:T(8,128)} %param.24) | copy-start | bytes 3145732
  78.0 157.6 %copy-start.19 = (f32[1,2048]{1,0:T(1,128)S(1)}, f32[1,2048]{1,0:T(1,128)}, u32[]{:S(2)}) copy-start(f32[1,2048]{1,0:T(1,128)} %copy-done.18) | copy-start | bytes 24580
  78.1 157.6 %copy-start.21 = (f32[1,2048]{1,0:T(1,128)S(1)}, f32[1,2048]{1,0:T(1,128)}, u32[]{:S(2)}) copy-start(f32[1,2048]{1,0:T(1,128)} %copy-done.20) | copy-start | bytes 24580
  78.1 157.6 %copy-start.30 = (f32[8]{0:T(128)S(1)}, f32[8]{0:T(128)}, u32[]{:S(2)}) copy-start(f32[8]{0:T(128)} %copy-done.29) | copy-start | bytes 100
  78.1 157.6 %copy-start.32 = (f32[8]{0:T(128)S(1)}, f32[8]{0:T(128)}, u32[]{:S(2)}) copy-start(f32[8]{0:T(128)} %copy-done.31) | copy-start | bytes 100
  78.1 157.6 %copy-start.34 = (f32[8]{0:T(128)S(1)}, f32[8]{0:T(128)}, u32[]{:S(2)}) copy-start(f32[8]{0:T(128)} %copy-done.33) | copy-start | bytes 100
  (5 other events, 5.3 us)
Sparse Core Ops, SparseCore 0:
  14.8 137.4 all-reduce.4
where the time goes:
time: 243 us; the launch traced here: 245 us
  blocking collectives  158 us (65%)
  other arithmetic  35.9 us (15%)
  local copies, waits for them, and re-layouts  18.1 us (7%)
  matrix products  17.1 us (7%)
  between operations  15.6 us (6%)
    unnamed x1, blocking collectives  152 us
    concatenate x4, other arithmetic, pair_matrix(): return jnp.concatenate([upper_half, lower_half], axis=0)  17.8 us
    dot_general x4, matrix products, highest_dot(): jnp.dot(left_side, right_side, precision=lax.Precision.HIGHEST, preferred...  10.6 us
    convert_element_type x1, other arithmetic, edge_message(): jax.nn.gelu(convolve(turned, sections[0]), approximate=False)  7.17 us
    all_gather x1, blocking collectives, body(): block_feats = lax.all_gather(atom_feats, 'tgt', axis=0, tiled=True)  5.96 us
    squeeze x4, local copies, waits for them, and re-layouts, pair_matrix(): weights[conv_index, 1]  5.04 us
  transfers between devices with their start and end apart: 1, of which 0 were waited for; matrix products, arithmetic and copies ran while one was open for 23% of the time, Pallas kernels for 0%

commit v1 on v0

v1 whole, which is shorter than its diff:
```python
import functools
import math

import jax
import jax.numpy as jnp
from jax import lax
from jax.experimental import pallas as pl
from jax.experimental.pallas import tpu as pltpu
from jax.sharding import PartitionSpec as P

MESH = pl.DeviceIdType.MESH
F32 = jnp.float32
BF16 = jnp.bfloat16
DEGREES = 4
ORDER_PLAN = (3, 1, 2, 0, 4)


def units_of(order):
    return (DEGREES + 2) // 2 if order == 0 else DEGREES + 1 - order


def first_unit(order):
    return sum(units_of(m) for m in range(order))


UNITS = first_unit(DEGREES + 1)


def first_block(order):
    return 0 if order == 0 else DEGREES + 1 + sum(2 * (DEGREES + 1 - m) for m in range(1, order))


def split(value):
    high = value.astype(BF16)
    return high, (value - high.astype(F32)).astype(BF16)


def half_turn(x):
    u = x * x
    s = x * (1 + u * (-1 / 6 + u * (1 / 120 + u * (-1 / 5040 + u * (1 / 362880 - u / 39916800)))))
    c = 1 + u * (
        -0.5
        + u * (1 / 24 + u * (-1 / 720 + u * (1 / 40320 + u * (-1 / 3628800 + u / 479001600))))
    )
    return 1 - 2 * s * s, 2 * s * c


def gelu(x):
    return 0.5 * x * (1 + lax.erf(x * math.sqrt(0.5)))


def dot(a, b):
    return jnp.dot(a, b, preferred_element_type=F32)


def kernel(
    sizes,
    x_ref, pos_ref, esrc_ref, etgt_ref, eang_ref, escale_ref, count_ref, kidx_ref, kfilt_hbm,
    w0_hbm, w1_hbm, w2_hbm, w3_hbm, w4_hbm,
    edge_out, long_out,
    xs, ew, w0, w1, w2, w3, w4, kfilt, y, e, t, h, send, recv,
    x_send, x_recv, ew_send, ew_recv, g_send, g_recv, w_sem,
):
    S, T, own, C, rows, sources, edges, kvecs = sizes
    N = S * T
    si, ti = lax.axis_index("src"), lax.axis_index("tgt")
    me = si * T + ti
    hbm = (w0_hbm, w1_hbm, w2_hbm, w3_hbm, w4_hbm)
    held = (w0, w1, w2, w3, w4)
    blocks = (DEGREES + 1) ** 2
    front = (blocks + 1) // 2

    weight_copies = []
    for conv in (0, 1):
        for m in range(DEGREES + 1):
            weight_copies.append(
                pltpu.make_async_copy(hbm[m].at[conv], held[m].at[conv], w_sem.at[conv, m])
            )
    for copy in weight_copies[: DEGREES + 1]:
        copy.start()
    filter_copy = pltpu.make_async_copy(kfilt_hbm, kfilt, w_sem.at[2, 0])

    barrier = pltpu.get_barrier_semaphore()

    def greet(d, _):
        p = lax.rem(me + d, N)
        pl.semaphore_signal(barrier, inc=1, device_id=(p // T, lax.rem(p, T)), device_id_type=MESH)
        return 0

    lax.fori_loop(1, N, greet, 0)

    xf = x_ref[...].astype(F32)
    tail = jnp.concatenate(
        [xf[:, front * C :], jnp.zeros((own, (2 * front - blocks) * C), F32)], axis=1
    )
    xs[ti] = jnp.concatenate([xf[:, : front * C], tail], axis=0).astype(BF16)
    lane = lax.broadcasted_iota(jnp.int32, (own, C), 1)
    diagonal = lax.broadcasted_iota(jnp.int32, (own, own), 0) == lax.broadcasted_iota(
        jnp.int32, (own, own), 1
    )
    placed = jnp.zeros((own, C), F32)
    own_columns = []
    for axis in range(3):
        column = jnp.sum(jnp.where(diagonal, pos_ref[axis : axis + 1, :], 0.0), axis=1, keepdims=True)
        own_columns.append(column)
        placed = jnp.where(lane == axis, column, placed)
    ew[me] = jnp.concatenate([xf[:, :C], placed], axis=0)

    pl.semaphore_wait(barrier, N - 1)

    def x_copy(slot, peer, there):
        return pltpu.make_async_remote_copy(
            src_ref=xs.at[slot], dst_ref=xs.at[slot], send_sem=x_send.at[peer],
            recv_sem=x_recv.at[there], device_id=(si, peer), device_id_type=MESH,
        )

    for d in range(1, T):
        x_copy(ti, lax.rem(ti + d, T), ti).start()

    def ew_copy(slot, p):
        return pltpu.make_async_remote_copy(
            src_ref=ew.at[slot], dst_ref=ew.at[slot], send_sem=ew_send.at[p],
            recv_sem=ew_recv.at[slot], device_id=(p // T, lax.rem(p, T)), device_id_type=MESH,
        )

    def ew_start(d, _):
        ew_copy(me, lax.rem(me + d, N)).start()
        return 0

    lax.fori_loop(1, N, ew_start, 0)
    for copy in weight_copies[DEGREES + 1 :]:
        copy.start()
    filter_copy.start()

    c1, s1 = half_turn(0.5 * eang_ref[...])
    c2, s2 = c1 * c1 - s1 * s1, 2 * s1 * c1
    c3, s3 = c2 * c1 - s2 * s1, s2 * c1 + c2 * s1
    c4, s4 = c2 * c2 - s2 * s2, 2 * s2 * c2
    cosines, sines = (None, c1, c2, c3, c4), (None, s1, s2, s3, s4)
    slots = lax.broadcasted_iota(jnp.int32, (1, edges), 1)
    scale = jnp.where(slots < count_ref[si, ti], escale_ref[...], 0.0)
    source_hot = lax.broadcasted_iota(jnp.int32, (sources, edges), 0) == esrc_ref[...]
    target_hot = lax.broadcasted_iota(jnp.int32, (rows, edges), 0) == etgt_ref[...]

    def put(hot, value):
        return jnp.where(hot, value, 0.0)

    def build_e(m):
        if m == 0:
            hot = put(source_hot, jnp.ones((1, edges), F32))
            parts = [hot, hot]
        else:
            ch, sh = cosines[m].astype(BF16).astype(F32), sines[m].astype(BF16).astype(F32)
            ch_hot, sh_hot = put(source_hot, ch), put(source_hot, sh)
            parts = [
                ch_hot, sh_hot, ch_hot, sh_hot,
                put(source_hot, cosines[m] - ch), put(source_hot, sines[m] - sh),
            ]
        depth = e.shape[1]
        used = len(parts) * sources
        if used < depth:
            parts.append(jnp.zeros((depth - used, edges), F32))
        e[...] = jnp.transpose(jnp.concatenate(parts, axis=0)).astype(BF16)

    def build_t(m):
        if m == 0:
            terms = [scale]
        else:
            terms = [scale * cosines[m], scale * sines[m]]
        count = len(terms)
        for i, term in enumerate(terms):
            high = term.astype(BF16).astype(F32)
            t[i * rows : (i + 1) * rows, :] = put(target_hot, high).astype(BF16)
            t[(count + i) * rows : (count + i + 1) * rows, :] = put(target_hot, term - high).astype(BF16)
        return count

    for d in range(1, T):
        peer = lax.rem(ti + d, T)
        x_copy(peer, peer, peer).wait_recv()
    for copy in weight_copies[: DEGREES + 1]:
        copy.wait()
    gathered = xs[...].astype(F32)

    def x_block(index):
        half, at = index // front, index % front
        piece = gathered[:, half * own : (half + 1) * own, at * C : (at + 1) * C]
        return piece.reshape(T * own, C)

    y[...] = jnp.zeros_like(y)
    for m in ORDER_PLAN:
        width = DEGREES + 1 - m
        base = first_block(m)
        if m == 0:
            left = jnp.concatenate([x_block(i) for i in range(width)], axis=1).astype(BF16)
            high, low = split(dot(left, w0[0]))
            for i in range(width):
                at = slice((i % 2) * C, (i % 2 + 1) * C)
                y[i // 2, 0:sources, at] = high[:, i * C : (i + 1) * C]
                y[i // 2, sources : 2 * sources, at] = low[:, i * C : (i + 1) * C]
        else:
            a = jnp.concatenate([x_block(base + i) for i in range(width)], axis=1)
            b = jnp.concatenate([x_block(base + width + i) for i in range(width)], axis=1)
            left = jnp.concatenate([a, b], axis=0).astype(BF16)
            by_w, by_v = dot(left, held[m][0, 0]), dot(left, held[m][0, 1])
            ya = by_w[:sources] - by_v[sources:]
            yb = by_v[:sources] + by_w[sources:]
            ah, al = split(ya)
            bh, bl = split(yb)
            for i in range(width):
                cut = slice(i * C, (i + 1) * C)
                unit = first_unit(m) + i
                for place, (p, q) in enumerate(
                    ((ah, bh), (bh, -ah), (al, bl), (bl, -al), (ah, bh), (bh, -ah))
                ):
                    at = slice(place * sources, (place + 1) * sources)
                    y[unit, at, 0:C] = p[:, cut]
                    y[unit, at, C : 2 * C] = q[:, cut]

    def g_copy(m, slot, p):
        span = pl.ds(first_unit(m), units_of(m))
        return pltpu.make_async_remote_copy(
            src_ref=send.at[p, span], dst_ref=recv.at[slot, span], send_sem=g_send.at[m, p],
            recv_sem=g_recv.at[m, slot], device_id=(p, ti), device_id_type=MESH,
        )

    step = 256
    for m in ORDER_PLAN:
        build_e(m)
        count = build_t(m)

        def one_unit(unit, _, count=count):
            for at in range(0, edges, step):
                h[at : at + step, :] = gelu(dot(e[at : at + step, :], y[unit])).astype(BF16)
            both = dot(t[0 : 2 * count * rows, :], h[...])
            total = both[: count * rows] + both[count * rows :]
            if count == 1:
                a, b = total[:, :C], total[:, C:]
            else:
                a = total[:rows, :C] - total[rows:, C:]
                b = total[:rows, C:] + total[rows:, :C]
            stacked = jnp.concatenate([a.reshape(S, own, C), b.reshape(S, own, C)], axis=1)
            send[:, pl.ds(unit, 1)] = stacked.astype(BF16)[:, None]
            return 0

        lax.fori_loop(first_unit(m), first_unit(m) + units_of(m), one_unit, 0)

        def g_start(d, _, m=m):
            g_copy(m, si, lax.rem(si + d, S)).start()
            return 0

        lax.fori_loop(1, S, g_start, 0)

    def ew_wait(d, _):
        p = lax.rem(me + d, N)
        copy = ew_copy(p, p)
        copy.wait_recv()
        return 0

    lax.fori_loop(1, N, ew_wait, 0)
    filter_copy.wait()
    k_step = 512
    some = math.gcd(N, 32)

    def tables(columns, at):
        turns = sum(
            column * kidx_ref[axis : axis + 1, pl.ds(at, k_step)].astype(F32)
            for axis, column in enumerate(columns)
        )
        return half_turn(math.pi * (turns - jnp.floor(turns + 0.5)))

    def k_chunk(number, total):
        at = pl.multiple_of(number * k_step, k_step)

        def atoms(group, carried):
            block = ew[pl.ds(group * some, some)]
            charges = jnp.transpose(block[:, :own].reshape(some * own, C)).astype(BF16)
            places = block[:, own:].reshape(some * own, C)
            made = tables([places[:, axis : axis + 1] for axis in range(3)], at)
            return tuple(
                held_sum + sum(dot(charges, part) for part in split(table))
                for held_sum, table in zip(carried, made)
            )

        zero = jnp.zeros((C, k_step), F32)
        if N == some:
            facts_here = atoms(0, (zero, zero))
        else:
            facts_here = lax.fori_loop(0, N // some, atoms, (zero, zero))
        filt = jnp.transpose(kfilt[pl.ds(at, k_step), :])
        for table, fact in zip(tables(own_columns, at), facts_here):
            th, tl = split(table)
            fh, fl = split(filt * fact)
            dims = (((1,), (1,)), ((), ()))
            for p, q in ((th, fh), (tl, fh), (th, fl)):
                total = total + lax.dot_general(p, q, dims, preferred_element_type=F32)
        return total

    summed = lax.fori_loop(0, kvecs // k_step, k_chunk, jnp.zeros((own, C), F32))
    long_out[...] = summed * (1.0 / math.sqrt(N * own * kvecs))

    for copy in weight_copies[DEGREES + 1 :]:
        copy.wait()
    for m in ORDER_PLAN:

        def g_wait(d, _, m=m):
            p = lax.rem(si + d, S)
            g_copy(m, p, p).wait_recv()
            return 0

        lax.fori_loop(1, S, g_wait, 0)
        span = pl.ds(first_unit(m), units_of(m))

        def g_add(d, total):
            return total + recv[lax.rem(si + d, S), span].astype(F32)

        total = lax.fori_loop(1, S, g_add, send[si, span].astype(F32))
        width = DEGREES + 1 - m
        base = first_block(m) * C
        if m == 0:
            left = jnp.concatenate(
                [total[i // 2, (i % 2) * own : (i % 2 + 1) * own] for i in range(width)], axis=1
            )
            by_w = dot(jnp.concatenate(split(left), axis=0), w0[1])
            edge_out[:, : width * C] = (by_w[:own] + by_w[own:]).astype(BF16)
        else:
            left = jnp.concatenate([total[i] for i in range(width)], axis=1)
            left = jnp.concatenate(split(left), axis=0)
            by_w, by_v = dot(left, held[m][1, 0]), dot(left, held[m][1, 1])
            by_w, by_v = (v[: 2 * own] + v[2 * own :] for v in (by_w, by_v))
            edge_out[:, base : base + width * C] = (by_w[:own] - by_v[own:]).astype(BF16)
            edge_out[:, base + width * C : base + 2 * width * C] = (by_v[:own] + by_w[own:]).astype(BF16)

    for d in range(1, T):
        peer = lax.rem(ti + d, T)
        x_copy(ti, peer, ti).wait_send()

    def ew_sent(d, _):
        ew_copy(me, lax.rem(me + d, N)).wait_send()
        return 0

    lax.fori_loop(1, N, ew_sent, 0)

    def g_sent(d, _):
        for m in ORDER_PLAN:
            g_copy(m, si, lax.rem(si + d, S)).wait_send()
        return 0

    lax.fori_loop(1, S, g_sent, 0)


def body(
    atom_feats, positions, edge_src, edge_tgt, edge_angle, edge_scale, edge_count, k_index, k_filter,
    weight_zero, weight_first, weight_second, weight_third, weight_fourth,
):
    S, T = lax.axis_size("src"), lax.axis_size("tgt")
    own, features = atom_feats.shape
    kvecs, C = k_filter.shape
    edges = edge_src.shape[0]
    rows, sources = own * S, own * T
    weights = (weight_zero, weight_first, weight_second, weight_third, weight_fourth)
    sizes = (S, T, own, C, rows, sources, edges, kvecs)
    depth = max(C, 6 * sources)
    front = ((DEGREES + 1) ** 2 + 1) // 2
    vmem = pl.BlockSpec(memory_space=pltpu.VMEM)
    smem = pl.BlockSpec(memory_space=pltpu.SMEM)
    anywhere = pl.BlockSpec(memory_space=pl.ANY)
    dma = pltpu.SemaphoreType.DMA
    row = lambda v: v.reshape(1, edges)
    return pl.pallas_call(
        functools.partial(kernel, sizes),
        out_shape=(
            jax.ShapeDtypeStruct((own, features), BF16),
            jax.ShapeDtypeStruct((own, C), F32),
        ),
        in_specs=[vmem] * 6 + [smem, vmem] + [anywhere] * 6,
        out_specs=(vmem, vmem),
        scratch_shapes=[
            pltpu.VMEM((T, 2 * own, front * C), BF16),
            pltpu.VMEM((S * T, 2 * own, C), F32),
            *[pltpu.VMEM(w.shape, BF16) for w in weights],
            pltpu.VMEM((kvecs, C), F32),
            pltpu.VMEM((UNITS, depth, 2 * C), BF16),
            pltpu.VMEM((edges, depth), BF16),
            pltpu.VMEM((4 * rows, edges), BF16),
            pltpu.VMEM((edges, 2 * C), BF16),
            pltpu.VMEM((S, UNITS, 2 * own, C), BF16),
            pltpu.VMEM((S, UNITS, 2 * own, C), BF16),
            dma((T,)), dma((T,)), dma((S * T,)), dma((S * T,)),
            dma((DEGREES + 1, S)), dma((DEGREES + 1, S)), dma((3, DEGREES + 1)),
        ],
        compiler_params=pltpu.CompilerParams(
            collective_id=0, has_side_effects=True, vmem_limit_bytes=56 * 1024 * 1024
        ),
    )(
        atom_feats, positions, row(edge_src), row(edge_tgt), row(edge_angle), row(edge_scale),
        edge_count, k_index, k_filter, *weights,
    )


def solution(mesh):
    both = P(("src", "tgt"))
    return jax.shard_map(
        body,
        mesh=mesh,
        in_specs=(
            P(("src", "tgt"), None), P(None, ("src", "tgt")), both, both, both, both,
            P(), P(), P(), P(), P(), P(), P(), P(),
        ),
        out_specs=(P(("tgt", "src"), None), P(("src", "tgt"), None)),
        check_vma=False,
    )
```

time: 243 us -> 41.9 us (0.17); the launches traced: 245 us -> 41.7 us
  blocking collectives: 158 us -> 0 us
  Pallas kernels: 0 us -> 37 us
  other arithmetic: 35.9 us -> 0 us
  matrix products: 17.1 us -> 0 us
  between operations: 15.6 us -> 0.64 us
  local copies, waits for them, and re-layouts: 18.1 us -> 4.05 us
    unnamed x1 -> x0, blocking collectives: 152 us -> none
    pallas_call x0 -> x1, Pallas kernels: none -> 37 us  [body(): pl.pallas_call(functools.partial(kernel, sizes), out_shape=(jax.ShapeDtyp...]
    concatenate x5 -> x0, other arithmetic: 18 us -> none  [the longest x4 17.8 us: pair_matrix(): return jnp.concatenate([upper_half, lower_half], axis=0)]
    dot_general x15 -> x0, matrix products: 17.1 us -> none  [the longest x4 10.6 us: highest_dot(): jnp.dot(left_side, right_side, precision=lax.Precision.HIGHEST, preferred...]
    convert_element_type x3 -> x0, other arithmetic: 9.09 us -> none  [the longest x1 7.17 us: edge_message(): jax.nn.gelu(convolve(turned, sections[0]), approximate=False)]
    squeeze x5 -> x0, local copies, waits for them, and re-layouts: 7.84 us -> none  [the longest x4 5.04 us: pair_matrix(): weights[conv_index, 1]]
    all_gather x1 -> x0, blocking collectives: 5.96 us -> none  [body(): block_feats = lax.all_gather(atom_feats, 'tgt', axis=0, tiled=True)]
    neg x4 -> x0, other arithmetic: 3.26 us -> none  [pair_matrix(): -weights[conv_index, 1]]
  transfers between devices with their start and end apart: 1 -> 0, of which waited for: 0 -> 0; matrix products, arithmetic and copies ran while one was open for 23% -> 0% of each run, Pallas kernels for 0% -> 0%
where the time goes in v1:
time: 41.9 us; the launch traced here: 41.7 us
  Pallas kernels  37 us (88%)
  local copies, waits for them, and re-layouts  4.05 us (10%)
  between operations  0.64 us (2%)
    pallas_call x1, Pallas kernels, body(): pl.pallas_call(functools.partial(kernel, sizes), out_shape=(jax.ShapeDtyp...  37 us
    unnamed x3, local copies, waits for them, and re-layouts  4.05 us

profile of v1, /device:TPU:0, one launch (start us, length us, event | category | flops | bytes accessed | tf_op | source)
XLA Modules:
  0.0 41.7 jit_solution(6854497644301724860)
XLA Ops:
  0.6 1.4 %copy.16.count_ref = s32[16,2]{1,0:T(8,128)} copy(s32[16,2]{0,1:T(2,128)} %param.20) | data formatting | bytes 256 | tf_op args[6]
  2.0 37.0 %shard_map.149 = (bf16[8,3200]{1,0:T(8,128)(2,1)}, f32[8,128]{1,0:T(8,128)}) custom-call(bf16[8,3200]{1,0:T(8,128)(2,1)} %x_ref.1, f32[3,8]{1,0:T(4,128)} %pos_ref.1, s32[1,1024]{1,0:T(1,128)} %bitcast.4, s32[1,1024]{1,0:T(1,128)} %bitcast.5, f32[1,1024]{1,0:T(1,128)} %bitcast.6, f32[1,1024]{1,0:T(1,128)} %bitcast.7, s32[16,2]{1,0:T(8,128)} %copy.16.count_ref, ...), custom_call_target="tpu_custom_call" | custom-call | tf_op jit(solution)/shard_map/pallas_call | solution.py:369
  39.0 1.4 %copy.19 = bf16[8,3200]{1,0:T(8,128)(2,1)} copy(bf16[8,3200]{1,0:T(8,128)(2,1)} %get-tuple-element.4) | data formatting | bytes 102400
  40.4 1.3 %copy.20 = f32[8,128]{1,0:T(8,128)} copy(f32[8,128]{1,0:T(8,128)} %get-tuple-element.5) | data formatting | bytes 8192

commit v2 on v1

--- a/solution.py
+++ b/solution.py
@@ -58,8 +58,8 @@
     x_ref, pos_ref, esrc_ref, etgt_ref, eang_ref, escale_ref, count_ref, kidx_ref, kfilt_hbm,
     w0_hbm, w1_hbm, w2_hbm, w3_hbm, w4_hbm,
     edge_out, long_out,
-    xs, ew, w0, w1, w2, w3, w4, kfilt, y, e, t, h, send, recv,
-    x_send, x_recv, ew_send, ew_recv, g_send, g_recv, w_sem,
+    xs, ew, w0, w1, w2, w3, w4, kfilt, y, e, t, h, parts, pair_in, paired, near_in, send, recv,
+    x_send, x_recv, ew_send, ew_recv, pair_send, pair_recv, near_send, near_recv, far_send, far_recv, w_sem,
 ):
     S, T, own, C, rows, sources, edges, kvecs = sizes
     N = S * T
@@ -82,12 +82,19 @@
 
     barrier = pltpu.get_barrier_semaphore()
 
-    def greet(d, _):
-        p = lax.rem(me + d, N)
-        pl.semaphore_signal(barrier, inc=1, device_id=(p // T, lax.rem(p, T)), device_id_type=MESH)
-        return 0
-
-    lax.fori_loop(1, N, greet, 0)
+    far_count = S // 4
+    core, near, far = lax.rem(si, 2), lax.rem(si // 2, 2), si // 4
+    pair_id, near_id = si + 1 - 2 * core, si + 2 - 4 * near
+
+    def far_id(p):
+        return p * 4 + near * 2 + core
+
+    tgt_peers = [lax.rem(ti + d, T) for d in range(1, T)]
+    far_peers = [lax.rem(far + d, far_count) for d in range(1, far_count)]
+    partners = [(si, p) for p in tgt_peers] + [(pair_id, ti), (near_id, ti)]
+    partners += [(far_id(p), ti) for p in far_peers]
+    for partner in partners:
+        pl.semaphore_signal(barrier, inc=1, device_id=partner, device_id_type=MESH)
 
     xf = x_ref[...].astype(F32)
     tail = jnp.concatenate(
@@ -106,7 +113,7 @@
         placed = jnp.where(lane == axis, column, placed)
     ew[me] = jnp.concatenate([xf[:, :C], placed], axis=0)
 
-    pl.semaphore_wait(barrier, N - 1)
+    pl.semaphore_wait(barrier, len(partners))
 
     def x_copy(slot, peer, there):
         return pltpu.make_async_remote_copy(
@@ -117,17 +124,27 @@
     for d in range(1, T):
         x_copy(ti, lax.rem(ti + d, T), ti).start()
 
-    def ew_copy(slot, p):
+    def ew_copy(device, mine, theirs, first, size):
         return pltpu.make_async_remote_copy(
-            src_ref=ew.at[slot], dst_ref=ew.at[slot], send_sem=ew_send.at[p],
-            recv_sem=ew_recv.at[slot], device_id=(p // T, lax.rem(p, T)), device_id_type=MESH,
-        )
-
-    def ew_start(d, _):
-        ew_copy(me, lax.rem(me + d, N)).start()
-        return 0
-
-    lax.fori_loop(1, N, ew_start, 0)
+            src_ref=ew.at[pl.ds(first, size)], dst_ref=ew.at[pl.ds(first, size)],
+            send_sem=ew_send.at[theirs], recv_sem=ew_recv.at[mine],
+            device_id=device, device_id_type=MESH,
+        )
+
+    def ew_tgt(p, slot, sem):
+        return ew_copy((si, p), sem, p, si * T + slot, 1)
+
+    def ew_pair(owner):
+        return ew_copy((pair_id, ti), T, T, owner * T, T)
+
+    def ew_near(owner):
+        return ew_copy((near_id, ti), T + 1, T + 1, (owner // 2) * 2 * T, 2 * T)
+
+    def ew_far(p, owner, sem):
+        return ew_copy((far_id(p), ti), T + 2 + sem, T + 2 + p, owner * 4 * T, 4 * T)
+
+    for p in tgt_peers:
+        ew_tgt(p, ti, ti).start()
     for copy in weight_copies[DEGREES + 1 :]:
         copy.start()
     filter_copy.start()
@@ -138,7 +155,7 @@
     c4, s4 = c2 * c2 - s2 * s2, 2 * s2 * c2
     cosines, sines = (None, c1, c2, c3, c4), (None, s1, s2, s3, s4)
     slots = lax.broadcasted_iota(jnp.int32, (1, edges), 1)
-    scale = jnp.where(slots < count_ref[si, ti], escale_ref[...], 0.0)
+    scale = jnp.where(slots < count_ref[ti, si], escale_ref[...], 0.0)
     source_hot = lax.broadcasted_iota(jnp.int32, (sources, edges), 0) == esrc_ref[...]
     target_hot = lax.broadcasted_iota(jnp.int32, (rows, edges), 0) == etgt_ref[...]
 
@@ -177,6 +194,9 @@
     for d in range(1, T):
         peer = lax.rem(ti + d, T)
         x_copy(peer, peer, peer).wait_recv()
+    for p in tgt_peers:
+        ew_tgt(p, p, p).wait_recv()
+    ew_pair(si).start()
     for copy in weight_copies[: DEGREES + 1]:
         copy.wait()
     gathered = xs[...].astype(F32)
@@ -216,15 +236,56 @@
                     y[unit, at, 0:C] = p[:, cut]
                     y[unit, at, C : 2 * C] = q[:, cut]
 
-    def g_copy(m, slot, p):
-        span = pl.ds(first_unit(m), units_of(m))
+    def span(m):
+        return pl.ds(first_unit(m), units_of(m))
+
+    def pair_copy(m):
         return pltpu.make_async_remote_copy(
-            src_ref=send.at[p, span], dst_ref=recv.at[slot, span], send_sem=g_send.at[m, p],
-            recv_sem=g_recv.at[m, slot], device_id=(p, ti), device_id_type=MESH,
-        )
+            src_ref=parts.at[:, 1 - core, span(m)], dst_ref=pair_in.at[:, span(m)],
+            send_sem=pair_send.at[m], recv_sem=pair_recv.at[m],
+            device_id=(pair_id, ti), device_id_type=MESH,
+        )
+
+    def near_copy(m):
+        return pltpu.make_async_remote_copy(
+            src_ref=paired.at[:, 1 - near, span(m)], dst_ref=near_in.at[:, span(m)],
+            send_sem=near_send.at[m], recv_sem=near_recv.at[m],
+            device_id=(near_id, ti), device_id_type=MESH,
+        )
+
+    def far_copy(m, slot, p):
+        return pltpu.make_async_remote_copy(
+            src_ref=send.at[p, span(m)], dst_ref=recv.at[slot, span(m)],
+            send_sem=far_send.at[m, p], recv_sem=far_recv.at[m, slot],
+            device_id=(far_id(p), ti), device_id_type=MESH,
+        )
+
+    def near_start(m):
+        pair_copy(m).wait_recv()
+
+        def add(i, _):
+            total = parts[i, core, span(m)].astype(F32) + pair_in[i, span(m)].astype(F32)
+            paired[i // 2, lax.rem(i, 2), span(m)] = total.astype(BF16)
+            return 0
+
+        lax.fori_loop(0, S // 2, add, 0)
+        near_copy(m).start()
+
+    def far_start(m):
+        near_copy(m).wait_recv()
+
+        def add(i, _):
+            total = paired[i, near, span(m)].astype(F32) + near_in[i, span(m)].astype(F32)
+            send[i, span(m)] = total.astype(BF16)
+            return 0
+
+        lax.fori_loop(0, far_count, add, 0)
+        for d in range(1, far_count):
+            p = lax.rem(far + d, far_count)
+            far_copy(m, far, p).start()
 
     step = 256
-    for m in ORDER_PLAN:
+    for turn, m in enumerate(ORDER_PLAN):
         build_e(m)
         count = build_t(m)
 
@@ -239,24 +300,26 @@
                 a = total[:rows, :C] - total[rows:, C:]
                 b = total[:rows, C:] + total[rows:, :C]
             stacked = jnp.concatenate([a.reshape(S, own, C), b.reshape(S, own, C)], axis=1)
-            send[:, pl.ds(unit, 1)] = stacked.astype(BF16)[:, None]
+            parts[:, :, pl.ds(unit, 1)] = stacked.astype(BF16).reshape(S // 2, 2, 1, 2 * own, C)
             return 0
 
         lax.fori_loop(first_unit(m), first_unit(m) + units_of(m), one_unit, 0)
 
-        def g_start(d, _, m=m):
-            g_copy(m, si, lax.rem(si + d, S)).start()
-            return 0
-
-        lax.fori_loop(1, S, g_start, 0)
-
-    def ew_wait(d, _):
-        p = lax.rem(me + d, N)
-        copy = ew_copy(p, p)
-        copy.wait_recv()
-        return 0
-
-    lax.fori_loop(1, N, ew_wait, 0)
+        pair_copy(m).start()
+        if turn == 0:
+            ew_pair(pair_id).wait_recv()
+            ew_near(si).start()
+        if turn == 1:
+            ew_near(near_id).wait_recv()
+            for p in far_peers:
+                ew_far(p, far, far).start()
+        if turn >= 1:
+            near_start(ORDER_PLAN[turn - 1])
+        if turn >= 2:
+            far_start(ORDER_PLAN[turn - 2])
+
+    for p in far_peers:
+        ew_far(p, p, p).wait_recv()
     filter_copy.wait()
     k_step = 512
     some = math.gcd(N, 32)
@@ -295,25 +358,24 @@
                 total = total + lax.dot_general(p, q, dims, preferred_element_type=F32)
         return total
 
-    summed = lax.fori_loop(0, kvecs // k_step, k_chunk, jnp.zeros((own, C), F32))
+    chunks = kvecs // k_step
+    summed = lax.fori_loop(0, chunks // 2, k_chunk, jnp.zeros((own, C), F32))
+    near_start(ORDER_PLAN[-1])
+    far_start(ORDER_PLAN[-2])
+    summed = lax.fori_loop(chunks // 2, chunks - chunks // 4, k_chunk, summed)
+    far_start(ORDER_PLAN[-1])
+    summed = lax.fori_loop(chunks - chunks // 4, chunks, k_chunk, summed)
     long_out[...] = summed * (1.0 / math.sqrt(N * own * kvecs))
 
     for copy in weight_copies[DEGREES + 1 :]:
         copy.wait()
     for m in ORDER_PLAN:
 
-        def g_wait(d, _, m=m):
-            p = lax.rem(si + d, S)
-            g_copy(m, p, p).wait_recv()
-            return 0
-
-        lax.fori_loop(1, S, g_wait, 0)
-        span = pl.ds(first_unit(m), units_of(m))
-
-        def g_add(d, total):
-            return total + recv[lax.rem(si + d, S), span].astype(F32)
-
-        total = lax.fori_loop(1, S, g_add, send[si, span].astype(F32))
+        total = send[far, span(m)].astype(F32)
+        for d in range(1, far_count):
+            p = lax.rem(far + d, far_count)
+            far_copy(m, p, p).wait_recv()
+            total = total + recv[p, span(m)].astype(F32)
         width = DEGREES + 1 - m
         base = first_block(m) * C
         if m == 0:
@@ -334,18 +396,22 @@
         peer = lax.rem(ti + d, T)
         x_copy(ti, peer, ti).wait_send()
 
-    def ew_sent(d, _):
-        ew_copy(me, lax.rem(me + d, N)).wait_send()
-        return 0
-
-    lax.fori_loop(1, N, ew_sent, 0)
-
-    def g_sent(d, _):
-        for m in ORDER_PLAN:
-            g_copy(m, si, lax.rem(si + d, S)).wait_send()
-        return 0
-
-    lax.fori_loop(1, S, g_sent, 0)
+    for p in tgt_peers:
+        ew_tgt(p, ti, ti).wait_send()
+    ew_pair(si).wait_send()
+    ew_near(si).wait_send()
+    for p in far_peers:
+        ew_far(p, far, far).wait_send()
+    for m in ORDER_PLAN:
+        pair_copy(m).wait_send()
+        near_copy(m).wait_send()
+        for d in range(1, far_count):
+            far_copy(m, far, lax.rem(far + d, far_count)).wait_send()
+
+
+def hand_on(edge_in, long_in, edge_out, long_out):
+    edge_out[...] = edge_in[...]
+    long_out[...] = long_in[...]
 
 
 def body(
@@ -366,7 +432,7 @@
     anywhere = pl.BlockSpec(memory_space=pl.ANY)
     dma = pltpu.SemaphoreType.DMA
     row = lambda v: v.reshape(1, edges)
-    return pl.pallas_call(
+    made = pl.pallas_call(
         functools.partial(kernel, sizes),
         out_shape=(
             jax.ShapeDtypeStruct((own, features), BF16),
@@ -383,18 +449,29 @@
             pltpu.VMEM((edges, depth), BF16),
             pltpu.VMEM((4 * rows, edges), BF16),
             pltpu.VMEM((edges, 2 * C), BF16),
-            pltpu.VMEM((S, UNITS, 2 * own, C), BF16),
-            pltpu.VMEM((S, UNITS, 2 * own, C), BF16),
-            dma((T,)), dma((T,)), dma((S * T,)), dma((S * T,)),
-            dma((DEGREES + 1, S)), dma((DEGREES + 1, S)), dma((3, DEGREES + 1)),
+            pltpu.VMEM((S // 2, 2, UNITS, 2 * own, C), BF16),
+            pltpu.VMEM((S // 2, UNITS, 2 * own, C), BF16),
+            pltpu.VMEM((S // 4, 2, UNITS, 2 * own, C), BF16),
+            pltpu.VMEM((S // 4, UNITS, 2 * own, C), BF16),
+            pltpu.VMEM((S // 4, UNITS, 2 * own, C), BF16),
+            pltpu.VMEM((S // 4, UNITS, 2 * own, C), BF16),
+            dma((T,)), dma((T,)), dma((T + 2 + S // 4,)), dma((T + 2 + S // 4,)),
+            *[dma((DEGREES + 1,)) for _ in range(4)],
+            dma((DEGREES + 1, S // 4)), dma((DEGREES + 1, S // 4)), dma((3, DEGREES + 1)),
         ],
         compiler_params=pltpu.CompilerParams(
             collective_id=0, has_side_effects=True, vmem_limit_bytes=56 * 1024 * 1024
         ),
     )(
         atom_feats, positions, row(edge_src), row(edge_tgt), row(edge_angle), row(edge_scale),
-        edge_count, k_index, k_filter, *weights,
+        edge_count.T, k_index, k_filter, *weights,
     )
+    return pl.pallas_call(
+        hand_on,
+        out_shape=tuple(jax.ShapeDtypeStruct(v.shape, v.dtype) for v in made),
+        in_specs=[vmem, vmem],
+        out_specs=(vmem, vmem),
+    )(*made)
 
 
 def solution(mesh):

time: 41.9 us -> 36.5 us (0.87)
  local copies, waits for them, and re-layouts: 4.05 us -> 0 us
  Pallas kernels: 37 us -> 35.6 us
    unnamed x3 -> x0, local copies, waits for them, and re-layouts: 4.05 us -> none
    pallas_call x1, Pallas kernels: 37 us -> 34.2 us  [body(): pl.pallas_call(functools.partial(kernel, sizes), out_shape=(jax.ShapeDtyp...]
    pallas_call x0 -> x1, Pallas kernels: none -> 1.43 us  [body(): pl.pallas_call(hand_on, out_shape=tuple((jax.ShapeDtypeStruct(v.shape, v....]
where the time goes in v2:
time: 36.5 us; the launch traced here: 36.2 us
  Pallas kernels  35.6 us (98%)
  between operations  0.64 us (2%)
    pallas_call x1, Pallas kernels, body(): pl.pallas_call(functools.partial(kernel, sizes), out_shape=(jax.ShapeDtyp...  34.2 us
    pallas_call x1, Pallas kernels, body(): pl.pallas_call(hand_on, out_shape=tuple((jax.ShapeDtypeStruct(v.shape, v....  1.43 us

profile of v2, /device:TPU:0, one launch (start us, length us, event | category | flops | bytes accessed | tf_op | source)
XLA Modules:
  0.0 36.2 jit_solution(17984838365091498413)
XLA Ops:
  0.6 34.2 %shard_map.149 = (bf16[8,3200]{1,0:T(8,128)(2,1)}, f32[8,128]{1,0:T(8,128)}) custom-call(bf16[8,3200]{1,0:T(8,128)(2,1)} %x_ref.1, f32[3,8]{1,0:T(4,128)} %pos_ref.1, s32[1,1024]{1,0:T(1,128)} %bitcast.5, s32[1,1024]{1,0:T(1,128)} %bitcast.6, f32[1,1024]{1,0:T(1,128)} %bitcast.7, f32[1,1024]{1,0:T(1,128)} %bitcast.8, s32[2,16]{1,0:T(2,128)} %bitcast.9, ...), custom_call_target="tpu_custom_call" | custom-call | tf_op jit(solution)/shard_map/pallas_call | solution.py:435
  34.8 1.4 %shard_map.150 = (bf16[8,3200]{1,0:T(8,128)(2,1)}, f32[8,128]{1,0:T(8,128)}) custom-call(bf16[8,3200]{1,0:T(8,128)(2,1)} %get-tuple-element.4.edge_in, f32[8,128]{1,0:T(8,128)} %get-tuple-element.5.long_in), custom_call_target="tpu_custom_call" | custom-call | tf_op jit(solution)/shard_map/pallas_call | solution.py:469
